TPU v7x, 32 devices: a whole 2x2x4 slice. The times are simulated.
32 devices in a mesh: grp: 2 (over y), tok: 4 (over x, core), feat: 4 (over z).
Axes of the slice: x: 2, y: 2, z: 4, core: 2. Of those that a mesh axis runs over, the one named last changes fastest.
Arguments:
- query_matrix_rows: bfloat16 [2048, 32, 128], P(('grp', 'tok'), 'feat'), parts along dimension 0, may hold values from -1.796875 to 1.796875
- key_matrix_rows: bfloat16 [2048, 2, 128], P(('grp', 'tok')), parts along dimension 0, may hold values from -1.796875 to 1.796875
- value_rows: bfloat16 [2048, 2, 128], P(('grp', 'tok')), parts along dimension 0, may hold values from -40 to 40
- incoming_state: float32 [4, 16384, 128], P('grp', 'feat'), parts along dimension 0, may hold values from -14 to 14
- out_gain: float32 [128], replicated, may hold values from 0.1 to 1.9
Outputs:
- attended: bfloat16 [2048, 32, 128], P(('grp', 'tok'), 'feat'), parts along dimension 0
There are 2 independent parts, one for each index of `grp`. A program takes and returns all parts, laid end to end along the dimension named above; an argument that names none is the same for every part. Nothing has to cross between parts.
All inputs are finite; a program needn't handle non-finite values.
Results may differ from a plain program's by a relative error of at most 0.0033.
Values may be sent and summed in bfloat16 or wider, within the bound.
A program may use at most 192 MiB of HBM per device.

v0:
```python
import jax
import jax.numpy as jnp
from jax import lax
from jax.sharding import PartitionSpec as P

QUERY_HEAD_COUNT = 32
KEY_VALUE_HEADS = 2


def entering(part, axis, combine, identity):
    place = lax.axis_index(axis)
    gathered = lax.all_gather(part, axis)
    state = jnp.zeros_like(part) + jnp.asarray(identity, part.dtype)

    def one(lap, state):
        return combine(state, lax.dynamic_index_in_dim(gathered, lap, 0, False))

    return lax.fori_loop(0, place, one, state)


def expand(matrix, offset, row_count):
    head_width = matrix.shape[2]
    matrix_f = matrix.astype(jnp.float32)
    picked = lax.dynamic_slice_in_dim(matrix_f, offset, row_count, 2)
    outer_prod = picked[..., :, None] * matrix_f[..., None, :]
    return outer_prod.reshape(matrix.shape[0], matrix.shape[1], row_count * head_width)


def add_states(earlier, later):
    return earlier + later


def local(query_matrix_rows, key_matrix_rows, value_rows, incoming_state, out_gain):
    tok_len, heads_dev, head_width = query_matrix_rows.shape
    kv_heads = key_matrix_rows.shape[1]
    feat_count = lax.axis_size("feat")
    slice_rows = head_width // feat_count
    slice_len = slice_rows * head_width
    group_count = QUERY_HEAD_COUNT // KEY_VALUE_HEADS
    feat_pos = lax.axis_index("feat")
    row_first = feat_pos * slice_rows
    kv_own = feat_pos * heads_dev // group_count
    key_own = lax.dynamic_index_in_dim(key_matrix_rows, kv_own, 1, keepdims=False)
    value_own = lax.dynamic_index_in_dim(value_rows, kv_own, 1, keepdims=False)
    scores = jnp.einsum(
        "thd,ud->htu", query_matrix_rows, key_own, preferred_element_type=jnp.float32
    )
    causal_mask = jnp.arange(tok_len)[:, None] >= jnp.arange(tok_len)[None, :]
    weights = jnp.where(causal_mask[None], scores * scores, 0.0).astype(jnp.bfloat16)
    local_read = jnp.einsum("htu,ue->the", weights, value_own, preferred_element_type=jnp.float32)
    empty_state = jnp.zeros((kv_heads, slice_len, head_width), jnp.float32)
    phi_key = expand(key_matrix_rows, row_first, slice_rows)
    window_prefix = entering(
        jnp.einsum(
            "tgf,tge->gfe", phi_key, value_rows.astype(jnp.float32), precision=lax.Precision.HIGHEST
        ),
        "tok",
        add_states,
        empty_state,
    )
    prefix = incoming_state + window_prefix
    query_all = lax.all_gather(query_matrix_rows, "feat", axis=1, tiled=True)
    head_count = lax.axis_size("feat") * heads_dev

    def one_block(block_id):
        head_first = block_id * heads_dev
        query_block = lax.dynamic_slice_in_dim(query_all, head_first, heads_dev, 1)
        phi_query = expand(query_block, row_first, slice_rows)
        state_part = lax.dynamic_index_in_dim(prefix, head_first // group_count, 0, keepdims=False)
        return jnp.einsum("thf,fe->hte", phi_query, state_part, precision=lax.Precision.HIGHEST)

    blocks = lax.map(one_block, jnp.arange(head_count // heads_dev, dtype=jnp.int32))
    owned = lax.psum_scatter(
        blocks.reshape(head_count, tok_len, head_width), "feat", scatter_dimension=0, tiled=True
    )
    carried = jnp.transpose(owned, (1, 0, 2))
    summed = local_read + carried
    mean_square = jnp.mean(summed * summed, axis=-1, keepdims=True)
    return (summed * lax.rsqrt(mean_square + 1e-06) * out_gain).astype(jnp.bfloat16)


def solution(mesh):
    return jax.shard_map(
        local,
        mesh=mesh,
        in_specs=(
            P(("grp", "tok"), "feat", None),
            P(("grp", "tok"), None, None),
            P(("grp", "tok"), None, None),
            P("grp", "feat", None),
            P(),
        ),
        out_specs=P(("grp", "tok"), "feat", None),
        check_vma=False,
    )
```

profile of v0, /device:TPU:18, one launch (start us, length us, event | category | flops | bytes accessed | tf_op | source)
XLA Modules:
  0.0 619.4 jit_solution(6732033997507156274)
XLA Ops:
  6.5 0.0 copy-start
  6.5 0.0 all-gather.6.cloned.1.call-start
  6.5 1.1 copy.28
  7.6 1.0 convert_element_type.17
  8.6 0.3 constant_dynamic-slice_fusion.1
  9.0 0.1 copy.27
  9.1 1.1 broadcast_multiply_fusion.1
  10.2 0.0 copy-done
  10.2 5.3 fusion.14
  15.5 0.0 copy-start.2
  15.5 0.0 all-gather.6.cloned.1.call-update
  15.5 0.0 all-gather.4.cloned.1.call-start
  15.6 1.0 copy-done.2
  16.5 0.9 copy.25
  17.4 0.0 all-gather.4.cloned.1.call-update
  17.4 0.0 reduce-scatter.2.cloned.1.call-start
  17.5 5.7 copy.30
  23.1 98.6 %all-gather.6.cloned.1.call-done = f32[8,4096,128]{2,1,0:T(8,128)} async-done(((f32[2,4096,128]{2,1,0:T(8,128)}), f32[8,4096,128]{2,1,0:T(8,128)}) %all-gather.6.cloned.1.call-update) | async-done | bytes 16777232 | tf_op jit(solution)/shard_map/all_gather | solution.py:12
  121.7 2.2 broadcast_in_dim.37
  123.9 12.1 %while.22 = (s32[]{:T(128)}, f32[2,4096,128]{2,1,0:T(8,128)}, s32[]{:T(128)}, f32[4,2,4096,128]{3,2,1,0:T(8,128)}, s32[]{:T(128)}, /*index=5*/s32[]{:T(128)}, s32[]{:T(128)}) while((s32[]{:T(128)}, f32[2,4096,128]{2,1,0:T(8,128)}, s32[]{:T(128)}, f32[4,2,4096,128]{3,2,1,0:T(8,128)}, s32[]{:T(128)}, /*index=5*/s32[]{:T(128)}, s32[]{:T(128)}) %tuple.52), condition=%wide.region_1.2_spmd, body=%wide.region_0.1_spmd.sunk | while | flops 1048581 | bytes 12583035 | solution.py:18
  123.9 5.8 bitcast_add_fusion.2
  129.8 6.2 %bitcast_add_fusion.2 = f32[2,4096,128]{2,1,0:T(8,128)} fusion(f32[2,4096,128]{2,1,0:T(8,128)} %get-tuple-element.205, f32[4,2,4096,128]{3,2,1,0:T(8,128)} %get-tuple-element.214, s32[]{:T(128)S(6)} %select_n.58), kind=kLoop, calls=%fused_computation.clone.1 | loop fusion | flops 1048576 | bytes 12582916 | tf_op jit(solution)/shard_map/while/body/add | solution.py:30
  136.0 5.7 copy.31
  141.7 6.1 add.66
  147.8 21.0 %all-gather.4.cloned.1.call-done = bf16[256,32,128]{2,0,1:T(8,128)(2,1)} async-done(((bf16[256,8,128]{2,0,1:T(8,128)(2,1)}), bf16[256,32,128]{2,0,1:T(8,128)(2,1)}) %all-gather.4.cloned.1.call-update) | async-done | bytes 2097168 | tf_op jit(solution)/shard_map/all_gather | solution.py:62
  168.8 363.4 %while.23 = (s32[]{:T(128)}, f32[4,8,256,128]{2,3,1,0:T(8,128)}, s32[4]{0:T(128)S(1)}, f32[2,4096,128]{1,2,0:T(8,128)}, bf16[256,32,128]{2,0,1:T(8,128)(2,1)}, /...) while((s32[]{:T(128)}, f32[4,8,256,128]{2,3,1,0:T(8,128)}, ...), condition=%wide.region_3.4_spmd, body=%wide.region_2.3_spmd.sunk | while | flops 12893552640 | bytes 140771744 | solution.py:72
  168.8 0.6 dynamic_slice.66
  170.1 1.1 dynamic-slice_convert_fusion.2
  171.2 0.3 constant_dynamic-slice_fusion.5
  171.5 11.5 %broadcast_multiply_fusion.3 = f32[256,8,32,128]{3,2,0,1:T(8,128)} fusion(f32[256,8,128]{2,0,1:T(8,128)S(1)} %dynamic-slice_convert_fusion.2, f32[256,8,32]{2,0,1:T(8,128)S(1)} %constant_dynamic-slice_fusion.5), kind=kLoop, calls=%fused_computation.1.clone.1 | loop fusion | flops 8388608 | bytes 34865152 | tf_op jit(solution)/shard_map/while/body/eval_jaxpr/mul | solution.py:25
  183.0 35.9 %mul.121 = f32[256,8,4096]{2,0,1:T(8,128)} reshape(f32[256,8,32,128]{3,2,0,1:T(8,128)} %broadcast_multiply_fusion.3) | data formatting | bytes 67108864 | tf_op jit(solution)/shard_map/while/body/eval_jaxpr/mul | solution.py:25
  218.9 40.8 %fusion.29 = f32[4,8,256,128]{2,3,1,0:T(8,128)} fusion(f32[4,8,256,128]{2,3,1,0:T(8,128)} %get-tuple-element.233, s32[]{:T(128)S(6)} %copy.57, f32[256,8,4096]{2,0,1:T(8,128)} %mul.121, f32[2,4096,128]{1,2,0:T(8,128)} %get-tuple-element.249, s32[]{:T(128)S(6)} %select_n.61), kind=kOutput, calls=%fused_computation.6.clone.1 | convolution fusion | flops 12884901888 | bytes 36700168 | tf_op jit(solution)/shard_map/while/body/eval_jaxpr/thf,fe->hte/dot_general | solution.py:70
  259.7 0.6 dynamic_slice.66
  260.9 1.1 dynamic-slice_convert_fusion.2
  262.0 0.3 constant_dynamic-slice_fusion.5
  262.4 11.5 %broadcast_multiply_fusion.3 = f32[256,8,32,128]{3,2,0,1:T(8,128)} fusion(f32[256,8,128]{2,0,1:T(8,128)S(1)} %dynamic-slice_convert_fusion.2, f32[256,8,32]{2,0,1:T(8,128)S(1)} %constant_dynamic-slice_fusion.5), kind=kLoop, calls=%fused_computation.1.clone.1 | loop fusion | flops 8388608 | bytes 34865152 | tf_op jit(solution)/shard_map/while/body/eval_jaxpr/mul | solution.py:25
  273.8 35.9 %mul.121 = f32[256,8,4096]{2,0,1:T(8,128)} reshape(f32[256,8,32,128]{3,2,0,1:T(8,128)} %broadcast_multiply_fusion.3) | data formatting | bytes 67108864 | tf_op jit(solution)/shard_map/while/body/eval_jaxpr/mul | solution.py:25
  309.7 40.8 %fusion.29 = f32[4,8,256,128]{2,3,1,0:T(8,128)} fusion(f32[4,8,256,128]{2,3,1,0:T(8,128)} %get-tuple-element.233, s32[]{:T(128)S(6)} %copy.57, f32[256,8,4096]{2,0,1:T(8,128)} %mul.121, f32[2,4096,128]{1,2,0:T(8,128)} %get-tuple-element.249, s32[]{:T(128)S(6)} %select_n.61), kind=kOutput, calls=%fused_computation.6.clone.1 | convolution fusion | flops 12884901888 | bytes 36700168 | tf_op jit(solution)/shard_map/while/body/eval_jaxpr/thf,fe->hte/dot_general | solution.py:70
  350.5 0.6 dynamic_slice.66
  351.8 1.1 dynamic-slice_convert_fusion.2
  352.9 0.3 constant_dynamic-slice_fusion.5
  353.2 11.5 %broadcast_multiply_fusion.3 = f32[256,8,32,128]{3,2,0,1:T(8,128)} fusion(f32[256,8,128]{2,0,1:T(8,128)S(1)} %dynamic-slice_convert_fusion.2, f32[256,8,32]{2,0,1:T(8,128)S(1)} %constant_dynamic-slice_fusion.5), kind=kLoop, calls=%fused_computation.1.clone.1 | loop fusion | flops 8388608 | bytes 34865152 | tf_op jit(solution)/shard_map/while/body/eval_jaxpr/mul | solution.py:25
  364.7 35.9 %mul.121 = f32[256,8,4096]{2,0,1:T(8,128)} reshape(f32[256,8,32,128]{3,2,0,1:T(8,128)} %broadcast_multiply_fusion.3) | data formatting | bytes 67108864 | tf_op jit(solution)/shard_map/while/body/eval_jaxpr/mul | solution.py:25
  400.6 40.8 %fusion.29 = f32[4,8,256,128]{2,3,1,0:T(8,128)} fusion(f32[4,8,256,128]{2,3,1,0:T(8,128)} %get-tuple-element.233, s32[]{:T(128)S(6)} %copy.57, f32[256,8,4096]{2,0,1:T(8,128)} %mul.121, f32[2,4096,128]{1,2,0:T(8,128)} %get-tuple-element.249, s32[]{:T(128)S(6)} %select_n.61), kind=kOutput, calls=%fused_computation.6.clone.1 | convolution fusion | flops 12884901888 | bytes 36700168 | tf_op jit(solution)/shard_map/while/body/eval_jaxpr/thf,fe->hte/dot_general | solution.py:70
  441.4 0.6 dynamic_slice.66
  442.6 1.1 dynamic-slice_convert_fusion.2
  443.8 0.3 constant_dynamic-slice_fusion.5
  444.1 11.5 %broadcast_multiply_fusion.3 = f32[256,8,32,128]{3,2,0,1:T(8,128)} fusion(f32[256,8,128]{2,0,1:T(8,128)S(1)} %dynamic-slice_convert_fusion.2, f32[256,8,32]{2,0,1:T(8,128)S(1)} %constant_dynamic-slice_fusion.5), kind=kLoop, calls=%fused_computation.1.clone.1 | loop fusion | flops 8388608 | bytes 34865152 | tf_op jit(solution)/shard_map/while/body/eval_jaxpr/mul | solution.py:25
  455.6 35.9 %mul.121 = f32[256,8,4096]{2,0,1:T(8,128)} reshape(f32[256,8,32,128]{3,2,0,1:T(8,128)} %broadcast_multiply_fusion.3) | data formatting | bytes 67108864 | tf_op jit(solution)/shard_map/while/body/eval_jaxpr/mul | solution.py:25
  491.4 40.8 %fusion.29 = f32[4,8,256,128]{2,3,1,0:T(8,128)} fusion(f32[4,8,256,128]{2,3,1,0:T(8,128)} %get-tuple-element.233, s32[]{:T(128)S(6)} %copy.57, f32[256,8,4096]{2,0,1:T(8,128)} %mul.121, f32[2,4096,128]{1,2,0:T(8,128)} %get-tuple-element.249, s32[]{:T(128)S(6)} %select_n.61), kind=kOutput, calls=%fused_computation.6.clone.1 | convolution fusion | flops 12884901888 | bytes 36700168 | tf_op jit(solution)/shard_map/while/body/eval_jaxpr/thf,fe->hte/dot_general | solution.py:70
  532.3 0.0 copy-start.1
  532.3 0.0 copy-start.3
  532.3 0.0 copy-start.4
  532.3 0.0 reduce-scatter.2.cloned.1.call-update
  532.3 0.1 constant_dynamic-slice_fusion.3
  532.5 0.1 copy.23
  532.6 0.5 copy-done.1
  533.2 0.1 constant_dynamic-slice_fusion.2
  533.3 76.5 %reduce-scatter.2.cloned.1.call-done = f32[8,256,128]{1,2,0:T(8,128)} async-done(((f32[32,256,128]{1,2,0:T(8,128)}), f32[8,256,128]{1,2,0:T(8,128)}) %reduce-scatter.2.cloned.1.call-update) | async-done | bytes 1048592 | tf_op jit(solution)/shard_map/reduce_scatter | solution.py:73
  609.8 0.0 copy-done.3
  609.8 1.8 multiply_reduce_fusion
  611.6 0.0 copy-done.4
  611.7 0.1 multiply_convert_fusion
  611.8 1.1 copy.33
  (4 shorter events, 0.0 us)
Async XLA Ops:
  6.5 3.6 copy-start
  6.5 115.2 %all-gather.6.cloned.1.call-start = ((), (), s32[]{:S(2)}) async-start(), calls=%async_computation.3 | async-start | bytes 20971520 | tf_op jit(solution)/shard_map/all_gather | solution.py:12
  15.5 1.0 copy-start.2
  15.5 153.3 %all-gather.4.cloned.1.call-start = ((), (), s32[]{:S(2)}) async-start(), calls=%async_computation.1 | async-start | bytes 2621440 | tf_op jit(solution)/shard_map/all_gather | solution.py:62
  17.4 592.4 %reduce-scatter.2.cloned.1.call-start = ((), (), s32[]{:S(2)}) async-start(), calls=%async_computation.2 | async-start | bytes 5242880 | tf_op jit(solution)/shard_map/reduce_scatter | solution.py:73
  532.3 0.9 copy-start.1
  532.3 77.5 %copy-start.3 = (bf16[256,8,128]{2,1,0:T(8,128)(2,1)S(1)}, bf16[256,8,128]{2,1,0:T(8,128)(2,1)}, u32[]{:S(2)}) copy-start(bf16[256,8,128]{2,1,0:T(8,128)(2,1)} %param.9) | copy-start | bytes 1572868
  532.3 79.4 %copy-start.4 = (f32[128]{0:T(128)S(1)}, f32[128]{0:T(128)}, u32[]{:S(2)}) copy-start(f32[128]{0:T(128)} %param.13) | copy-start | bytes 1540
Sparse Core Ops, SparseCore 0:
  15.6 106.0 all-gather.5
  123.3 45.4 all-gather.3
  532.4 77.3 reduce-scatter.1
where the time goes:
time: 625 us; the launch traced here: 619 us
  waiting for transfers between devices  196 us (31%)
  matrix products  170 us (27%)
  local copies, waits for them, and re-layouts  166 us (27%)
  other arithmetic  70.7 us (11%)
  between operations  13.2 us (2%)
    dot_general x4, matrix products, one_block(): jnp.einsum('thf,fe->hte', phi_query, state_part, precision=lax.Precision....  163 us
    mul x4, local copies, waits for them, and re-layouts, expand(): outer_prod = picked[..., :, None] * matrix_f[..., None, :]  144 us
    all_gather x1, waiting for transfers between devices, entering(): gathered = lax.all_gather(part, axis)  98.6 us
    reduce_scatter x1, waiting for transfers between devices, local(): lax.psum_scatter(blocks.reshape(head_count, tok_len, head_width), 'feat',...  76.5 us
    mul x5, other arithmetic, expand(): outer_prod = picked[..., :, None] * matrix_f[..., None, :]  46.9 us
    all_gather x1, waiting for transfers between devices, local(): query_all = lax.all_gather(query_matrix_rows, 'feat', axis=1, tiled=True)  21 us
  transfers between devices with their start and end apart: 3, of which 3 were waited for; matrix products, arithmetic and copies ran while one was open for 5% of the time, Pallas kernels for 0%

commit v1 on v0

v1 whole, which is shorter than its diff:
```python
import functools

import jax
import jax.numpy as jnp
from jax import lax
from jax.experimental import pallas as pl
from jax.experimental.pallas import tpu as pltpu
from jax.sharding import PartitionSpec as P

QUERY_HEAD_COUNT = 32
KEY_VALUE_HEADS = 2
MESH = pl.DeviceIdType.MESH


def flip(place, bit):
    return place + bit - 2 * bit * ((place // bit) % 2)


def kernel(
    n_feat, n_tok, heads_dev, row_tile,
    q_ref, kv_ref, state_ref, gain_ref, out_ref,
    state_all, send_buf, kv_all, acc,
    z_send, z_recv, f_send, f_recv, kv_send, kv_recv,
):
    z = lax.axis_index("feat")
    t = lax.axis_index("tok")
    group = QUERY_HEAD_COUNT // KEY_VALUE_HEADS
    rows, head = q_ref.shape
    slice_len = state_all.shape[1]
    slice_rows = slice_len // head
    piece = slice_len // n_tok
    tiles = rows // row_tile
    keys = kv_ref.shape[1]
    bits = []
    while 2 ** len(bits) < n_tok:
        bits.append(n_tok // 2 ** (len(bits) + 1))

    barrier = pltpu.get_barrier_semaphore()
    for step in range(1, n_feat):
        pl.semaphore_signal(
            barrier, inc=1, device_id={"feat": lax.rem(z + step, n_feat)}, device_id_type=MESH
        )
    for step in range(1, n_tok):
        pl.semaphore_signal(
            barrier, inc=1, device_id={"tok": lax.rem(t + step, n_tok)}, device_id_type=MESH
        )

    first = pl.multiple_of(t * piece, piece)
    for g in range(KEY_VALUE_HEADS):
        send_buf[g] = state_ref[g, pl.ds(first, piece), :].astype(jnp.bfloat16)

    pl.semaphore_wait(barrier, n_feat + n_tok - 2)

    pending = []
    z_copies = []
    for step in range(1, n_feat):
        peer = lax.rem(z + step, n_feat)
        copy = pltpu.make_async_remote_copy(
            src_ref=send_buf.at[peer * heads_dev // group],
            dst_ref=state_all.at[z, pl.ds(first, piece), :],
            send_sem=z_send.at[step - 1],
            recv_sem=z_recv.at[step - 1],
            device_id={"feat": peer},
            device_id_type=MESH,
        )
        copy.start()
        pending.append(copy)
        z_copies.append(copy)
    kv_copies = []
    for step in range(1, n_tok):
        copy = pltpu.make_async_remote_copy(
            src_ref=kv_ref,
            dst_ref=kv_all.at[t],
            send_sem=kv_send.at[step - 1],
            recv_sem=kv_recv.at[step - 1],
            device_id={"tok": lax.rem(t + step, n_tok)},
            device_id_type=MESH,
        )
        copy.start()
        pending.append(copy)
        kv_copies.append(copy)

    state_all[z] = state_ref[z * heads_dev // group].astype(jnp.bfloat16)

    def tile_loop(body):
        def one(tile, carry):
            body(pl.multiple_of(tile * row_tile, row_tile))
            return carry

        lax.fori_loop(0, tiles, one, 0)

    def read_slice(source, begin):
        shift = lax.rem(head - source * slice_rows, head)

        def one(row):
            q = q_ref[pl.ds(row, row_tile), :]
            turned = pltpu.roll(q.astype(jnp.float32), shift, 1).astype(jnp.bfloat16)
            total = None
            span = min(8, slice_rows)
            for a in range(0, slice_rows, span):
                phi = jnp.concatenate([turned[:, a + i : a + i + 1] * q for i in range(span)], axis=1)
                term = jnp.dot(
                    phi,
                    state_all[source, a * head : (a + span) * head, :],
                    preferred_element_type=jnp.float32,
                )
                total = term if total is None else total + term
            if begin:
                acc[pl.ds(row, row_tile), :] = total
            else:
                acc[pl.ds(row, row_tile), :] += total

        tile_loop(one)

    def attend(k_ref, v_ref, causal):
        def one(row):
            q = q_ref[pl.ds(row, row_tile), :]
            scores = lax.dot_general(
                q, k_ref[...], (((1,), (1,)), ((), ())), preferred_element_type=jnp.float32
            )
            weights = scores * scores
            if causal:
                place = row + lax.broadcasted_iota(jnp.int32, (row_tile, keys), 0)
                key = lax.broadcasted_iota(jnp.int32, (row_tile, keys), 1)
                weights = jnp.where(key * heads_dev <= place, weights, 0.0)
            acc[pl.ds(row, row_tile), :] += jnp.dot(
                weights.astype(jnp.bfloat16), v_ref[...], preferred_element_type=jnp.float32
            )

        tile_loop(one)

    forwards = {}

    def forward(step, source, stage):
        count = 2 ** stage
        for i in range(count):
            held = t
            for j in range(stage):
                if (i >> j) % 2:
                    held = flip(held, bits[j])
            where = state_all.at[source, pl.ds(pl.multiple_of(held * piece, piece), piece), :]
            slot = (step - 1) * (n_tok - 1) + count - 1 + i
            copy = pltpu.make_async_remote_copy(
                src_ref=where,
                dst_ref=where,
                send_sem=f_send.at[slot],
                recv_sem=f_recv.at[slot],
                device_id={"tok": flip(t, bits[stage])},
                device_id_type=MESH,
            )
            copy.start()
            pending.append(copy)
            forwards.setdefault((step, stage), []).append(copy)

    read_slice(z, True)
    stages = len(bits)
    for tick in range(n_feat - 1 + stages):
        if tick == min(1, n_feat - 2 + stages):
            attend(kv_ref.at[0], kv_ref.at[1], True)
        if tick == min(2, n_feat - 2 + stages):
            for copy in kv_copies:
                copy.wait_recv()

            def far(block, carry):
                attend(kv_all.at[block, 0], kv_all.at[block, 1], False)
                return carry

            lax.fori_loop(0, t, far, 0)
        ready = []
        for step in range(1, n_feat):
            stage = tick - (step - 1)
            source = lax.rem(z - step + n_feat, n_feat)
            if stage < 0 or stage > stages:
                continue
            if stage == 0:
                z_copies[step - 1].wait_recv()
            else:
                for copy in forwards[(step, stage - 1)]:
                    copy.wait_recv()
            if stage < stages:
                forward(step, source, stage)
            else:
                ready.append(source)
        for source in ready:
            read_slice(source, False)

    def finish(row):
        summed = acc[pl.ds(row, row_tile), :]
        mean_square = jnp.mean(summed * summed, axis=-1, keepdims=True)
        out_ref[pl.ds(row, row_tile), :] = (
            summed * lax.rsqrt(mean_square + 1e-06) * gain_ref[...]
        ).astype(jnp.bfloat16)

    tile_loop(finish)
    for copy in pending:
        copy.wait_send()


def local(query_matrix_rows, key_matrix_rows, value_rows, incoming_state, out_gain):
    tok_len, heads_dev, head = query_matrix_rows.shape
    n_feat = lax.axis_size("feat")
    n_tok = lax.axis_size("tok")
    kv_heads, slice_len, _ = incoming_state.shape
    rows = tok_len * heads_dev
    own = lax.axis_index("feat") * heads_dev // (QUERY_HEAD_COUNT // KEY_VALUE_HEADS)
    kv = jnp.stack(
        [
            lax.dynamic_index_in_dim(key_matrix_rows, own, 1, keepdims=False),
            lax.dynamic_index_in_dim(value_rows, own, 1, keepdims=False),
        ]
    )
    row_tile = min(512, rows)
    vmem = pl.BlockSpec(memory_space=pltpu.VMEM)
    out = pl.pallas_call(
        functools.partial(kernel, n_feat, n_tok, heads_dev, row_tile),
        out_shape=jax.ShapeDtypeStruct((rows, head), jnp.bfloat16),
        in_specs=[vmem] * 4,
        out_specs=vmem,
        scratch_shapes=[
            pltpu.VMEM((n_feat, slice_len, head), jnp.bfloat16),
            pltpu.VMEM((kv_heads, slice_len // n_tok, head), jnp.bfloat16),
            pltpu.VMEM((n_tok, 2, tok_len, head), jnp.bfloat16),
            pltpu.VMEM((rows, head), jnp.float32),
            pltpu.SemaphoreType.DMA((n_feat - 1,)),
            pltpu.SemaphoreType.DMA((n_feat - 1,)),
            pltpu.SemaphoreType.DMA(((n_feat - 1) * (n_tok - 1),)),
            pltpu.SemaphoreType.DMA(((n_feat - 1) * (n_tok - 1),)),
            pltpu.SemaphoreType.DMA((n_tok - 1,)),
            pltpu.SemaphoreType.DMA((n_tok - 1,)),
        ],
        compiler_params=pltpu.CompilerParams(
            collective_id=0, has_side_effects=True, vmem_limit_bytes=40 * 2**20
        ),
    )(query_matrix_rows.reshape(rows, head), kv, incoming_state, out_gain.reshape(1, head))
    return out.reshape(tok_len, heads_dev, head)


def solution(mesh):
    return jax.shard_map(
        local,
        mesh=mesh,
        in_specs=(
            P(("grp", "tok"), "feat", None),
            P(("grp", "tok"), None, None),
            P(("grp", "tok"), None, None),
            P("grp", "feat", None),
            P(),
        ),
        out_specs=P(("grp", "tok"), "feat", None),
        check_vma=False,
    )
```

time: 625 us -> 61.9 us (0.10)
  waiting for transfers between devices: 196 us -> 0 us
  matrix products: 170 us -> 0 us
  local copies, waits for them, and re-layouts: 166 us -> 5.94 us
  other arithmetic: 70.7 us -> 0.02 us
  Pallas kernels: 0 us -> 55.7 us
  between operations: 13.2 us -> 0.05 us
    dot_general x6 -> x0, matrix products: 170 us -> none  [the longest x4 163 us: one_block(): jnp.einsum('thf,fe->hte', phi_query, state_part, precision=lax.Precision....]
    mul x4 -> x0, local copies, waits for them, and re-layouts: 144 us -> none  [expand(): outer_prod = picked[..., :, None] * matrix_f[..., None, :]]
    all_gather x2 -> x0, waiting for transfers between devices: 120 us -> none  [the longest x1 98.6 us: entering(): gathered = lax.all_gather(part, axis)]
    reduce_scatter x1 -> x0, waiting for transfers between devices: 76.5 us -> none  [local(): lax.psum_scatter(blocks.reshape(head_count, tok_len, head_width), 'feat',...]
    pallas_call x0 -> x1, Pallas kernels: none -> 55.7 us  [local(): pl.pallas_call(functools.partial(kernel, n_feat, n_tok, heads_dev, row_ti...]
    mul x5 -> x0, other arithmetic: 46.9 us -> none  [expand(): outer_prod = picked[..., :, None] * matrix_f[..., None, :]]
    add x3 -> x0, other arithmetic: 18.2 us -> none  [the longest x2 12.1 us: add_states(): return earlier + later]
  transfers between devices with their start and end apart: 3 -> 0, of which waited for: 3 -> 0; matrix products, arithmetic and copies ran while one was open for 5% -> 0% of each run, Pallas kernels for 0% -> 0%
where the time goes in v1:
time: 61.9 us; the launch traced here: 61.7 us
  Pallas kernels  55.7 us (90%)
  local copies, waits for them, and re-layouts  5.94 us (10%)
    pallas_call x1, Pallas kernels, local(): pl.pallas_call(functools.partial(kernel, n_feat, n_tok, heads_dev, row_ti...  55.7 us
    unnamed x9, local copies, waits for them, and re-layouts  4.7 us
    dynamic_slice x1, local copies, waits for them, and re-layouts, local(): lax.dynamic_index_in_dim(value_rows, own, 1, keepdims=False)  1.24 us

profile of v1, /device:TPU:18, one launch (start us, length us, event | category | flops | bytes accessed | tf_op | source)
XLA Modules:
  0.0 61.7 jit_solution(10777397300418034962)
XLA Ops:
  0.0 1.2 %constant_dynamic-slice_fusion = (bf16[256,1,128]{2,1,0:T(2,128)(2,1)S(1)}, bf16[256,1,128]{2,1,0:T(2,128)(2,1)S(1)}) fusion(bf16[256,2,128]{2,1,0:T(2,128)(2,1)} %param.7, s32[]{:T(128)S(6)} %select_n.11, bf16[256,2,128]{2,1,0:T(2,128)(2,1)} %param.6), kind=kLoop, calls=%fused_computation.3 | loop fusion | bytes 262148 | tf_op jit(solution)/shard_map/jit(dynamic_index_in_dim)/dynamic_slice | solution.py:209
  1.3 0.0 copy-start
  1.3 2.2 %copy-done = f32[2,4096,128]{2,1,0:T(8,128)S(1)} copy-done((f32[2,4096,128]{2,1,0:T(8,128)S(1)}, f32[2,4096,128]{2,1,0:T(8,128)}, u32[]{:S(2)}) %copy-start) | copy-done | bytes 4194328
  3.5 0.0 copy-start.1
  3.5 1.0 %copy-done.1 = bf16[256,8,128]{2,1,0:T(8,128)(2,1)S(1)} copy-done((bf16[256,8,128]{2,1,0:T(8,128)(2,1)S(1)}, bf16[256,8,128]{2,1,0:T(8,128)(2,1)}, u32[]{:S(2)}) %copy-start.1) | copy-done | bytes 524312
  4.5 0.0 copy-start.2
  4.5 0.7 %copy-done.2 = f32[128]{0:T(128)S(1)} copy-done((f32[128]{0:T(128)S(1)}, f32[128]{0:T(128)}, u32[]{:S(2)}) %copy-start.2) | copy-done | bytes 536
  5.2 55.7 %shard_map.55 = bf16[2048,128]{1,0:T(8,128)(2,1)S(1)} custom-call(bf16[2048,128]{1,0:T(8,128)(2,1)S(1)} %bitcast.10, bf16[2,256,128]{2,1,0:T(8,128)(2,1)S(1)} %pad_maximum_fusion.kv_ref, f32[2,4096,128]{2,1,0:T(8,128)S(1)} %copy-done, f32[1,128]{1,0:T(1,128)S(1)} %bitcast.11), custom_call_target="tpu_custom_call" | custom-call | tf_op jit(solution)/shard_map/pallas_call | solution.py:214
  60.9 0.8 %copy.15 = bf16[256,8,128]{2,1,0:T(8,128)(2,1)} copy(bf16[256,8,128]{2,1,0:T(8,128)(2,1)S(1)} %bitcast.9) | data formatting | bytes 1048576
  (3 shorter events, 0.0 us)
Async XLA Ops:
  1.3 2.2 %copy-start = (f32[2,4096,128]{2,1,0:T(8,128)S(1)}, f32[2,4096,128]{2,1,0:T(8,128)}, u32[]{:S(2)}) copy-start(f32[2,4096,128]{2,1,0:T(8,128)} %state_ref.1) | copy-start | bytes 12582916
  3.5 1.0 %copy-start.1 = (bf16[256,8,128]{2,1,0:T(8,128)(2,1)S(1)}, bf16[256,8,128]{2,1,0:T(8,128)(2,1)}, u32[]{:S(2)}) copy-start(bf16[256,8,128]{2,1,0:T(8,128)(2,1)} %param.5) | copy-start | bytes 1572868
  4.5 0.7 %copy-start.2 = (f32[128]{0:T(128)S(1)}, f32[128]{0:T(128)}, u32[]{:S(2)}) copy-start(f32[128]{0:T(128)} %param.9) | copy-start | bytes 1540

commit v2 on v1

--- a/solution.py
+++ b/solution.py
@@ -17,10 +17,10 @@
 
 
 def kernel(
-    n_feat, n_tok, heads_dev, row_tile,
+    n_feat, n_tok, heads_dev, row_tile, cuts,
     q_ref, kv_ref, state_ref, gain_ref, out_ref,
-    state_all, send_buf, kv_all, acc,
-    z_send, z_recv, f_send, f_recv, kv_send, kv_recv,
+    state_all, send_wide, send_buf, own_wide, kv_all, acc,
+    in_sem, z_send, z_recv, f_send, f_recv, kv_send, kv_recv,
 ):
     z = lax.axis_index("feat")
     t = lax.axis_index("tok")
@@ -28,13 +28,25 @@
     rows, head = q_ref.shape
     slice_len = state_all.shape[1]
     slice_rows = slice_len // head
+    tiles = rows // row_tile
     piece = slice_len // n_tok
-    tiles = rows // row_tile
+    cut = piece // cuts
+    unit = max(1, tiles // 2)
     keys = kv_ref.shape[1]
     bits = []
     while 2 ** len(bits) < n_tok:
         bits.append(n_tok // 2 ** (len(bits) + 1))
 
+    first = pl.multiple_of(t * piece, piece)
+    own = z * heads_dev // group
+    members = group // heads_dev
+    for g in range(KEY_VALUE_HEADS):
+        pltpu.make_async_copy(
+            state_ref.at[g, pl.ds(first, piece), :], send_wide.at[g], in_sem.at[g]
+        ).start()
+    own_copy = pltpu.make_async_copy(state_ref.at[own], own_wide, in_sem.at[KEY_VALUE_HEADS])
+    own_copy.start()
+
     barrier = pltpu.get_barrier_semaphore()
     for step in range(1, n_feat):
         pl.semaphore_signal(
@@ -45,27 +57,45 @@
             barrier, inc=1, device_id={"tok": lax.rem(t + step, n_tok)}, device_id_type=MESH
         )
 
-    first = pl.multiple_of(t * piece, piece)
     for g in range(KEY_VALUE_HEADS):
-        send_buf[g] = state_ref[g, pl.ds(first, piece), :].astype(jnp.bfloat16)
+        pltpu.make_async_copy(
+            state_ref.at[g, pl.ds(first, piece), :], send_wide.at[g], in_sem.at[g]
+        ).wait()
+        send_buf[g] = send_wide[g].astype(jnp.bfloat16)
 
     pl.semaphore_wait(barrier, n_feat + n_tok - 2)
 
     pending = []
-    z_copies = []
-    for step in range(1, n_feat):
-        peer = lax.rem(z + step, n_feat)
-        copy = pltpu.make_async_remote_copy(
-            src_ref=send_buf.at[peer * heads_dev // group],
-            dst_ref=state_all.at[z, pl.ds(first, piece), :],
-            send_sem=z_send.at[step - 1],
-            recv_sem=z_recv.at[step - 1],
+
+    def along(source, c, src_ref, sem, peer):
+        return pltpu.make_async_remote_copy(
+            src_ref=src_ref,
+            dst_ref=state_all.at[source, pl.ds(first + c * cut, cut), :],
+            send_sem=sem,
+            recv_sem=z_recv.at[source * cuts + c],
             device_id={"feat": peer},
             device_id_type=MESH,
         )
-        copy.start()
-        pending.append(copy)
-        z_copies.append(copy)
+
+    for c in range(cuts):
+        piece_of = lambda g: send_buf.at[g, pl.ds(c * cut, cut), :]
+        for step in range(1, n_feat):
+            peer = lax.rem(z + step, n_feat)
+            copy = along(z, c, piece_of(peer // members), z_send.at[(step - 1) * cuts + c], peer)
+            copy.start()
+            pending.append(copy)
+    upper = 2 * z >= n_feat
+    mirrored = jnp.where(upper, n_feat - 1 - z, z)
+
+    def source_of(step):
+        near = jnp.where(step - 1 < mirrored, step - 1, step)
+        return jnp.where(upper, n_feat - 1 - near, near)
+
+    def pass_on(step, c):
+        source = source_of(step)
+        here = state_all.at[source, pl.ds(first + c * cut, cut), :]
+        along(source, c, here, z_send.at[(step - 1) * cuts + c], source).wait_recv()
+
     kv_copies = []
     for step in range(1, n_tok):
         copy = pltpu.make_async_remote_copy(
@@ -80,23 +110,24 @@
         pending.append(copy)
         kv_copies.append(copy)
 
-    state_all[z] = state_ref[z * heads_dev // group].astype(jnp.bfloat16)
-
-    def tile_loop(body):
+    own_copy.wait()
+    state_all[z] = own_wide[...].astype(jnp.bfloat16)
+
+    def tile_loop(body, begin=0, end=tiles):
         def one(tile, carry):
             body(pl.multiple_of(tile * row_tile, row_tile))
             return carry
 
-        lax.fori_loop(0, tiles, one, 0)
-
-    def read_slice(source, begin):
+        lax.fori_loop(begin, end, one, 0)
+
+    def read_slice(source, begin, tile, count):
         shift = lax.rem(head - source * slice_rows, head)
 
         def one(row):
             q = q_ref[pl.ds(row, row_tile), :]
             turned = pltpu.roll(q.astype(jnp.float32), shift, 1).astype(jnp.bfloat16)
             total = None
-            span = min(8, slice_rows)
+            span = min(32, slice_rows)
             for a in range(0, slice_rows, span):
                 phi = jnp.concatenate([turned[:, a + i : a + i + 1] * q for i in range(span)], axis=1)
                 term = jnp.dot(
@@ -110,7 +141,7 @@
             else:
                 acc[pl.ds(row, row_tile), :] += total
 
-        tile_loop(one)
+        tile_loop(one, tile, tile + count)
 
     def attend(k_ref, v_ref, causal):
         def one(row):
@@ -131,15 +162,15 @@
 
     forwards = {}
 
-    def forward(step, source, stage):
+    def forward(item, source, c, stage):
         count = 2 ** stage
         for i in range(count):
             held = t
             for j in range(stage):
                 if (i >> j) % 2:
                     held = flip(held, bits[j])
-            where = state_all.at[source, pl.ds(pl.multiple_of(held * piece, piece), piece), :]
-            slot = (step - 1) * (n_tok - 1) + count - 1 + i
+            where = state_all.at[source, pl.ds(pl.multiple_of(held * piece + c * cut, cut), cut), :]
+            slot = item * (n_tok - 1) + count - 1 + i
             copy = pltpu.make_async_remote_copy(
                 src_ref=where,
                 dst_ref=where,
@@ -150,39 +181,48 @@
             )
             copy.start()
             pending.append(copy)
-            forwards.setdefault((step, stage), []).append(copy)
-
-    read_slice(z, True)
+            forwards.setdefault((item, stage), []).append(copy)
+
+    def earlier_blocks():
+        for copy in kv_copies:
+            copy.wait_recv()
+
+        def far(block, carry):
+            attend(kv_all.at[block, 0], kv_all.at[block, 1], False)
+            return carry
+
+        lax.fori_loop(0, t, far, 0)
+
+    def own_block():
+        attend(kv_ref.at[0], kv_ref.at[1], True)
+
+    work = [functools.partial(read_slice, z, True, tile, unit) for tile in range(0, tiles, unit)]
+    work += [own_block, earlier_blocks]
     stages = len(bits)
-    for tick in range(n_feat - 1 + stages):
-        if tick == min(1, n_feat - 2 + stages):
-            attend(kv_ref.at[0], kv_ref.at[1], True)
-        if tick == min(2, n_feat - 2 + stages):
-            for copy in kv_copies:
-                copy.wait_recv()
-
-            def far(block, carry):
-                attend(kv_all.at[block, 0], kv_all.at[block, 1], False)
-                return carry
-
-            lax.fori_loop(0, t, far, 0)
-        ready = []
-        for step in range(1, n_feat):
-            stage = tick - (step - 1)
-            source = lax.rem(z - step + n_feat, n_feat)
-            if stage < 0 or stage > stages:
+    items = [(step, c) for step in range(1, n_feat) for c in range(cuts)]
+    for tick in range(len(items) + stages):
+        if work:
+            work.pop(0)()
+        for stage in range(stages + 1):
+            item = tick - stage
+            if item < 0 or item >= len(items):
                 continue
+            step, c = items[item]
+            source = source_of(step)
             if stage == 0:
-                z_copies[step - 1].wait_recv()
+                pass_on(step, c)
             else:
-                for copy in forwards[(step, stage - 1)]:
+                for copy in forwards[(item, stage - 1)]:
                     copy.wait_recv()
             if stage < stages:
-                forward(step, source, stage)
-            else:
-                ready.append(source)
-        for source in ready:
-            read_slice(source, False)
+                forward(item, source, c, stage)
+            elif c == cuts - 1:
+                work += [
+                    functools.partial(read_slice, source, False, tile, unit)
+                    for tile in range(0, tiles, unit)
+                ]
+    for piece_of_work in work:
+        piece_of_work()
 
     def finish(row):
         summed = acc[pl.ds(row, row_tile), :]
@@ -210,21 +250,25 @@
         ]
     )
     row_tile = min(512, rows)
+    cuts = max(1, 32 // (n_feat * n_tok))
     vmem = pl.BlockSpec(memory_space=pltpu.VMEM)
     out = pl.pallas_call(
-        functools.partial(kernel, n_feat, n_tok, heads_dev, row_tile),
+        functools.partial(kernel, n_feat, n_tok, heads_dev, row_tile, cuts),
         out_shape=jax.ShapeDtypeStruct((rows, head), jnp.bfloat16),
-        in_specs=[vmem] * 4,
+        in_specs=[vmem, vmem, pl.BlockSpec(memory_space=pltpu.HBM), vmem],
         out_specs=vmem,
         scratch_shapes=[
             pltpu.VMEM((n_feat, slice_len, head), jnp.bfloat16),
+            pltpu.VMEM((kv_heads, slice_len // n_tok, head), jnp.float32),
             pltpu.VMEM((kv_heads, slice_len // n_tok, head), jnp.bfloat16),
+            pltpu.VMEM((slice_len, head), jnp.float32),
             pltpu.VMEM((n_tok, 2, tok_len, head), jnp.bfloat16),
             pltpu.VMEM((rows, head), jnp.float32),
-            pltpu.SemaphoreType.DMA((n_feat - 1,)),
-            pltpu.SemaphoreType.DMA((n_feat - 1,)),
-            pltpu.SemaphoreType.DMA(((n_feat - 1) * (n_tok - 1),)),
-            pltpu.SemaphoreType.DMA(((n_feat - 1) * (n_tok - 1),)),
+            pltpu.SemaphoreType.DMA((kv_heads + 1,)),
+            pltpu.SemaphoreType.DMA(((n_feat - 1) * cuts,)),
+            pltpu.SemaphoreType.DMA((n_feat * cuts,)),
+            pltpu.SemaphoreType.DMA(((n_feat - 1) * (n_tok - 1) * cuts,)),
+            pltpu.SemaphoreType.DMA(((n_feat - 1) * (n_tok - 1) * cuts,)),
             pltpu.SemaphoreType.DMA((n_tok - 1,)),
             pltpu.SemaphoreType.DMA((n_tok - 1,)),
         ],

time: 61.9 us -> 57.4 us (0.927)
  Pallas kernels: 55.7 us -> 51.2 us
    pallas_call x1, Pallas kernels: 55.7 us -> 51.2 us  [local(): pl.pallas_call(functools.partial(kernel, n_feat, n_tok, heads_dev, row_ti...]
where the time goes in v2:
time: 57.4 us; the launch traced here: 57.2 us
  Pallas kernels  51.2 us (89%)
  local copies, waits for them, and re-layouts  5.94 us (10%)
    pallas_call x1, Pallas kernels, local(): pl.pallas_call(functools.partial(kernel, n_feat, n_tok, heads_dev, row_ti...  51.2 us
    unnamed x9, local copies, waits for them, and re-layouts  4.7 us
    dynamic_slice x1, local copies, waits for them, and re-layouts, local(): lax.dynamic_index_in_dim(value_rows, own, 1, keepdims=False)  1.24 us

profile of v2, /device:TPU:18, one launch (start us, length us, event | category | flops | bytes accessed | tf_op | source)
XLA Modules:
  0.0 57.2 jit_solution(16070196827245031219)
XLA Ops:
  0.0 1.2 %constant_dynamic-slice_fusion = (bf16[256,1,128]{2,1,0:T(2,128)(2,1)S(1)}, bf16[256,1,128]{2,1,0:T(2,128)(2,1)S(1)}) fusion(bf16[256,2,128]{2,1,0:T(2,128)(2,1)} %param.7, s32[]{:T(128)S(6)} %select_n.11, bf16[256,2,128]{2,1,0:T(2,128)(2,1)} %param.6), kind=kLoop, calls=%fused_computation.3 | loop fusion | bytes 262148 | tf_op jit(solution)/shard_map/jit(dynamic_index_in_dim)/dynamic_slice | solution.py:249
  1.3 0.0 copy-start
  1.3 2.2 %copy-done = f32[2,4096,128]{2,1,0:T(8,128)S(1)} copy-done((f32[2,4096,128]{2,1,0:T(8,128)S(1)}, f32[2,4096,128]{2,1,0:T(8,128)}, u32[]{:S(2)}) %copy-start) | copy-done | bytes 4194328
  3.5 0.0 copy-start.1
  3.5 1.0 %copy-done.1 = bf16[256,8,128]{2,1,0:T(8,128)(2,1)S(1)} copy-done((bf16[256,8,128]{2,1,0:T(8,128)(2,1)S(1)}, bf16[256,8,128]{2,1,0:T(8,128)(2,1)}, u32[]{:S(2)}) %copy-start.1) | copy-done | bytes 524312
  4.5 0.0 copy-start.2
  4.5 0.7 %copy-done.2 = f32[128]{0:T(128)S(1)} copy-done((f32[128]{0:T(128)S(1)}, f32[128]{0:T(128)}, u32[]{:S(2)}) %copy-start.2) | copy-done | bytes 536
  5.2 51.2 %shard_map.55 = bf16[2048,128]{1,0:T(8,128)(2,1)S(1)} custom-call(bf16[2048,128]{1,0:T(8,128)(2,1)S(1)} %bitcast.10, bf16[2,256,128]{2,1,0:T(8,128)(2,1)S(1)} %pad_maximum_fusion.kv_ref, f32[2,4096,128]{2,1,0:T(8,128)S(1)} %copy-done, f32[1,128]{1,0:T(1,128)S(1)} %bitcast.11), custom_call_target="tpu_custom_call" | custom-call | tf_op jit(solution)/shard_map/pallas_call | solution.py:255
  56.4 0.8 %copy.15 = bf16[256,8,128]{2,1,0:T(8,128)(2,1)} copy(bf16[256,8,128]{2,1,0:T(8,128)(2,1)S(1)} %bitcast.9) | data formatting | bytes 1048576
  (3 shorter events, 0.0 us)
Async XLA Ops:
  1.3 2.2 %copy-start = (f32[2,4096,128]{2,1,0:T(8,128)S(1)}, f32[2,4096,128]{2,1,0:T(8,128)}, u32[]{:S(2)}) copy-start(f32[2,4096,128]{2,1,0:T(8,128)} %state_ref.1) | copy-start | bytes 12582916
  3.5 1.0 %copy-start.1 = (bf16[256,8,128]{2,1,0:T(8,128)(2,1)S(1)}, bf16[256,8,128]{2,1,0:T(8,128)(2,1)}, u32[]{:S(2)}) copy-start(bf16[256,8,128]{2,1,0:T(8,128)(2,1)} %param.5) | copy-start | bytes 1572868
  4.5 0.7 %copy-start.2 = (f32[128]{0:T(128)S(1)}, f32[128]{0:T(128)}, u32[]{:S(2)}) copy-start(f32[128]{0:T(128)} %param.9) | copy-start | bytes 1540

commit v3 on v2

--- a/solution.py
+++ b/solution.py
@@ -106,8 +106,7 @@
             device_id={"tok": lax.rem(t + step, n_tok)},
             device_id_type=MESH,
         )
-        copy.start()
-        pending.append(copy)
+        pl.when(t + step < n_tok)(copy.start)
         kv_copies.append(copy)
 
     own_copy.wait()
@@ -184,8 +183,8 @@
             forwards.setdefault((item, stage), []).append(copy)
 
     def earlier_blocks():
-        for copy in kv_copies:
-            copy.wait_recv()
+        for step, copy in enumerate(kv_copies, 1):
+            pl.when(t >= step)(copy.wait_recv)
 
         def far(block, carry):
             attend(kv_all.at[block, 0], kv_all.at[block, 1], False)
@@ -234,6 +233,8 @@
     tile_loop(finish)
     for copy in pending:
         copy.wait_send()
+    for step, copy in enumerate(kv_copies, 1):
+        pl.when(t + step < n_tok)(copy.wait_send)
 
 
 def local(query_matrix_rows, key_matrix_rows, value_rows, incoming_state, out_gain):

time: 57.4 us -> 57.4 us (level)
  no operation moved by 1% of the time
where the time goes in v3:
time: 57.4 us; the launch traced here: 57.2 us
  Pallas kernels  51.2 us (89%)
  local copies, waits for them, and re-layouts  5.94 us (10%)
    pallas_call x1, Pallas kernels, local(): pl.pallas_call(functools.partial(kernel, n_feat, n_tok, heads_dev, row_ti...  51.2 us
    unnamed x9, local copies, waits for them, and re-layouts  4.7 us
    dynamic_slice x1, local copies, waits for them, and re-layouts, local(): lax.dynamic_index_in_dim(value_rows, own, 1, keepdims=False)  1.24 us

profile of v3, /device:TPU:18, one launch (start us, length us, event | category | flops | bytes accessed | tf_op | source)
XLA Modules:
  0.0 57.2 jit_solution(8968143193791681339)
XLA Ops:
  0.0 1.2 %constant_dynamic-slice_fusion = (bf16[256,1,128]{2,1,0:T(2,128)(2,1)S(1)}, bf16[256,1,128]{2,1,0:T(2,128)(2,1)S(1)}) fusion(bf16[256,2,128]{2,1,0:T(2,128)(2,1)} %param.7, s32[]{:T(128)S(6)} %select_n.11, bf16[256,2,128]{2,1,0:T(2,128)(2,1)} %param.6), kind=kLoop, calls=%fused_computation.3 | loop fusion | bytes 262148 | tf_op jit(solution)/shard_map/jit(dynamic_index_in_dim)/dynamic_slice | solution.py:250
  1.3 0.0 copy-start
  1.3 2.2 %copy-done = f32[2,4096,128]{2,1,0:T(8,128)S(1)} copy-done((f32[2,4096,128]{2,1,0:T(8,128)S(1)}, f32[2,4096,128]{2,1,0:T(8,128)}, u32[]{:S(2)}) %copy-start) | copy-done | bytes 4194328
  3.5 0.0 copy-start.1
  3.5 1.0 %copy-done.1 = bf16[256,8,128]{2,1,0:T(8,128)(2,1)S(1)} copy-done((bf16[256,8,128]{2,1,0:T(8,128)(2,1)S(1)}, bf16[256,8,128]{2,1,0:T(8,128)(2,1)}, u32[]{:S(2)}) %copy-start.1) | copy-done | bytes 524312
  4.5 0.0 copy-start.2
  4.5 0.7 %copy-done.2 = f32[128]{0:T(128)S(1)} copy-done((f32[128]{0:T(128)S(1)}, f32[128]{0:T(128)}, u32[]{:S(2)}) %copy-start.2) | copy-done | bytes 536
  5.2 51.2 %shard_map.55 = bf16[2048,128]{1,0:T(8,128)(2,1)S(1)} custom-call(bf16[2048,128]{1,0:T(8,128)(2,1)S(1)} %bitcast.10, bf16[2,256,128]{2,1,0:T(8,128)(2,1)S(1)} %pad_maximum_fusion.kv_ref, f32[2,4096,128]{2,1,0:T(8,128)S(1)} %copy-done, f32[1,128]{1,0:T(1,128)S(1)} %bitcast.11), custom_call_target="tpu_custom_call" | custom-call | tf_op jit(solution)/shard_map/pallas_call | solution.py:256
  56.4 0.8 %copy.15 = bf16[256,8,128]{2,1,0:T(8,128)(2,1)} copy(bf16[256,8,128]{2,1,0:T(8,128)(2,1)S(1)} %bitcast.9) | data formatting | bytes 1048576
  (3 shorter events, 0.0 us)
Async XLA Ops:
  1.3 2.2 %copy-start = (f32[2,4096,128]{2,1,0:T(8,128)S(1)}, f32[2,4096,128]{2,1,0:T(8,128)}, u32[]{:S(2)}) copy-start(f32[2,4096,128]{2,1,0:T(8,128)} %state_ref.1) | copy-start | bytes 12582916
  3.5 1.0 %copy-start.1 = (bf16[256,8,128]{2,1,0:T(8,128)(2,1)S(1)}, bf16[256,8,128]{2,1,0:T(8,128)(2,1)}, u32[]{:S(2)}) copy-start(bf16[256,8,128]{2,1,0:T(8,128)(2,1)} %param.5) | copy-start | bytes 1572868
  4.5 0.7 %copy-start.2 = (f32[128]{0:T(128)S(1)}, f32[128]{0:T(128)}, u32[]{:S(2)}) copy-start(f32[128]{0:T(128)} %param.9) | copy-start | bytes 1540
